TPU v7x, 32 devices: a whole 2x2x4 slice. The times are simulated.
32 devices in a mesh: tm: 8 (over z, core), bat: 4 (over y, x).
Axes of the slice: x: 2, y: 2, z: 4, core: 2. Of those that a mesh axis runs over, the one named last changes fastest.
Arguments:
- power0: float32 [128, 1536], P('tm', 'bat'), may hold values from -0.5 to 0.5
- charge0: float32 [128, 1536], P('tm', 'bat'), may hold values from 0 to 1
- dyn_dual0: float32 [128, 1536], P('tm', 'bat'), may hold values from -3 to 3
- feeder_dual0: float32 [128, 768], P(('tm', 'bat')), may hold values from 0 to 0.5
- price: float32 [128, 1536], P('tm', 'bat'), may hold values from -12 to 12
- inflow: float32 [128, 1536], P('tm', 'bat'), may hold values from -1.5 to 1.5
- power_limit: float32 [1536], P('bat'), may hold values from 0.5 to 6
- capacity: float32 [1536], P('bat'), may hold values from 0.5 to 8
- feeder_limit: float32 [768], replicated, may hold values from 0 to 1
- block_values: float32 [18, 128, 128], replicated, may hold values from -0.3125 to 0.3125
- block_cols: int32 [18], replicated, may hold values from 0 to 11, as said below
- block_offsets: int32 [7], replicated, may hold values from 0 to 18, as said below
Outputs:
- power: float32 [128, 1536], P('tm', 'bat')
- charge: float32 [128, 1536], P('tm', 'bat')
- dyn_dual: float32 [128, 1536], P('tm', 'bat')
- feeder_dual: float32 [128, 768], P(('tm', 'bat'))
Inputs may be any that keep to these rules, and one draw needn't show every extreme that they name: `block_cols`: every battery block 0 to 11 appears at least once. block_offsets[0] = 0, strictly rising, block_offsets[6] = 18.
All inputs are finite; a program needn't handle non-finite values.
Results may differ from a plain program's by a relative error of at most 0.0001.
Values sent between devices are 32-bit elements; how exact they have to be, the bound alone decides.
A program may use at most 64 MiB of HBM per device.

v0:
```python
import jax
import jax.numpy as jnp
from jax import lax
from jax.sharding import PartitionSpec as P

ITERS = 4


HIGH = lax.Precision.HIGHEST
ETA_STEP = 0.4
EPS_NORM = 1e-06


def shifted(block, axis, distance):
    devices = range(lax.axis_size(axis))
    route = [(i - distance, i) for i in devices if i - distance in devices]
    return lax.ppermute(block, axis, route)


def row_table(block_offsets, count):
    index_all = jnp.arange(count, dtype=jnp.int32)
    row_of = jnp.sum((index_all[:, None] >= block_offsets[None, 1:-1]).astype(jnp.int32), axis=1)
    feed_count = block_offsets.shape[0] - 1
    return (row_of[:, None] == jnp.arange(feed_count, dtype=jnp.int32)[None, :]).astype(jnp.float32)


def feeder_apply(field, block_values, rows_tab, cols_tab):
    count_rows = field.shape[0]
    blk = block_values.shape[1]
    blocks = field.reshape(count_rows, -1, blk)
    picked = jnp.einsum("rnk,jn->rjk", blocks, cols_tab, precision=HIGH)
    partial_rows = jnp.einsum("rjk,jmk->rjm", picked, block_values, precision=HIGH)
    summed = jnp.einsum("rjm,jf->rfm", partial_rows, rows_tab, precision=HIGH)
    return summed.reshape(count_rows, -1)


def feeder_adjoint(duals, block_values, rows_tab, cols_tab):
    count_rows = duals.shape[0]
    blk = block_values.shape[1]
    blocks = duals.reshape(count_rows, -1, blk)
    chosen = jnp.einsum("rfm,jf->rjm", blocks, rows_tab, precision=HIGH)
    pushed = jnp.einsum("rjm,jmk->rjk", chosen, block_values, precision=HIGH)
    spread = jnp.einsum("rjk,jn->rnk", pushed, cols_tab, precision=HIGH)
    return spread.reshape(count_rows, -1)


def shards(
    power0,
    charge0,
    dyn_dual0,
    feeder_dual0,
    price,
    inflow,
    power_limit,
    capacity,
    feeder_limit,
    block_values,
    block_cols,
    block_offsets,
):
    blk = block_values.shape[1]
    rows_tab = row_table(block_offsets, block_values.shape[0])
    local_batteries = power0.shape[1]
    local_blocks = local_batteries // blk
    first_block = lax.axis_index("bat") * local_blocks
    inside = (block_cols >= first_block) & (block_cols < first_block + local_blocks)
    local_cols = jnp.clip(block_cols - first_block, 0, local_blocks - 1)
    local_tab = (
        (local_cols[:, None] == jnp.arange(local_blocks, dtype=jnp.int32)[None, :])
        & inside[:, None]
    ).astype(jnp.float32)

    def couple_backward(duals):
        return feeder_adjoint(
            lax.all_gather(duals, "bat", axis=0, tiled=True), block_values, rows_tab, local_tab
        )

    power, charge, dyn_dual, feeder_dual = (power0, charge0, dyn_dual0, feeder_dual0)
    weight = jnp.asarray(1.0, dtype=jnp.float32)
    pushed = couple_backward(feeder_dual)
    limit_row = power_limit[None, :]
    for iteration in range(ITERS):
        step_primal = ETA_STEP / weight
        step_dual = ETA_STEP * weight
        following = shifted(dyn_dual[:1], "tm", -1)
        dual_next = jnp.concatenate([dyn_dual[1:], following], axis=0)
        power_new = jnp.clip(
            power - step_primal * (price - dyn_dual + pushed), -limit_row, limit_row
        )
        charge_new = jnp.clip(charge - step_primal * (dyn_dual - dual_next), 0.0, capacity[None, :])
        power_bar = 2.0 * power_new - power
        charge_bar = 2.0 * charge_new - charge
        last_iteration = iteration + 1 == ITERS
        if not last_iteration:
            move_power = power_new - power
            move_charge = charge_new - charge
            primal_local = jnp.sum(move_power * move_power + move_charge * move_charge)
            primal_sq = lax.psum(primal_local, ("tm", "bat"))
        coupled = lax.psum_scatter(
            feeder_apply(power_bar, block_values, rows_tab, local_tab),
            "bat",
            scatter_dimension=0,
            tiled=True,
        )
        preceding = shifted(charge_bar[-1:], "tm", 1)
        charge_prev = jnp.concatenate([preceding, charge_bar[:-1]], axis=0)
        dyn_new = dyn_dual + step_dual * (charge_bar - charge_prev - power_bar - inflow)
        feeder_new = jnp.maximum(0.0, feeder_dual + step_dual * (coupled - feeder_limit[None, :]))
        if not last_iteration:
            move_dyn = dyn_new - dyn_dual
            move_feed = feeder_new - feeder_dual
            dual_local = jnp.sum(move_dyn * move_dyn) + jnp.sum(move_feed * move_feed)
            dual_sq = lax.psum(dual_local, ("tm", "bat"))
            weight = jnp.sqrt(weight * jnp.sqrt((dual_sq + EPS_NORM) / (primal_sq + EPS_NORM)))
            pushed = couple_backward(feeder_new)
        power, charge, dyn_dual, feeder_dual = (power_new, charge_new, dyn_new, feeder_new)
    return (power, charge, dyn_dual, feeder_dual)


def solution(mesh):
    return jax.shard_map(
        shards,
        mesh=mesh,
        in_specs=(
            P("tm", "bat"),
            P("tm", "bat"),
            P("tm", "bat"),
            P(("tm", "bat"), None),
            P("tm", "bat"),
            P("tm", "bat"),
            P("bat"),
            P("bat"),
            P(),
            P(),
            P(),
            P(),
        ),
        out_specs=(P("tm", "bat"), P("tm", "bat"), P("tm", "bat"), P(("tm", "bat"), None)),
        check_vma=False,
    )
```

profile of v0, /device:TPU:0, one launch (start us, length us, event | category | flops | bytes accessed | tf_op | source)
XLA Modules:
  0.0 278.5 jit_solution(833112439892875416)
XLA Ops:
  0.7 0.8 slice.53
  1.5 1.3 collective-permute-start
  2.8 0.7 subtract_clamp_fusion
  3.5 0.7 compare_and_fusion
  4.1 0.7 slice.51
  4.8 0.1 convert_reduce_fusion
  4.9 9.8 %all-gather = f32[4,4,768]{2,1,0:T(4,128)S(1)} all-gather(f32[1,4,768]{2,1,0:T(4,128)} %bitcast.168), channel_id=1, replica_groups=mesh['tm'=8,'bat'=4] {'bat'}, dimensions={0}, use_global_device_ids=true | all-gather | bytes 61440 | tf_op jit(solution)/shard_map/all_gather | solution.py:75
  14.8 0.3 convolution_bitcast_fusion.7
  15.1 1.1 convolution_bitcast_fusion.15
  16.2 0.2 fusion.14
  16.5 0.6 add_reduce_fusion.2
  17.2 1.3 collective-permute-start.1
  18.5 0.6 dynamic-slice
  19.8 0.6 multiply_reduce_fusion.2
  20.4 0.3 convolution_bitcast_fusion.3
  20.7 1.9 convolution_bitcast_fusion.14
  22.7 0.2 fusion.12
  22.9 15.7 %all-reduce = f32[16,768]{1,0:T(8,128)S(1)} all-reduce(f32[16,768]{1,0:T(8,128)S(1)} %bitcast.158), channel_id=2, replica_groups=mesh['tm'=8,'bat'=4] {'bat'}, use_global_device_ids=true, to_apply=%region_2.3.clone | all-reduce | flops 12288 | bytes 98304
  38.6 0.6 multiply_reduce_fusion.5
  39.3 8.1 %all-gather.1 = f32[4,4,768]{2,1,0:T(4,128)S(1)} all-gather(f32[1,4,768]{2,1,0:T(4,128)S(1)} %bitcast.167), channel_id=1, replica_groups=mesh['tm'=8,'bat'=4] {'bat'}, dimensions={0}, use_global_device_ids=true | all-gather | bytes 61440 | tf_op jit(solution)/shard_map/all_gather | solution.py:75
  47.4 0.3 convolution_bitcast_fusion.6
  47.7 1.1 convolution_bitcast_fusion.13
  48.8 1.3 collective-permute-start.2
  50.1 0.2 fusion.10
  51.6 43.3 %all-reduce.6 = (f32[]{:T(128)}, f32[]{:T(128)}) all-reduce(f32[]{:T(128)S(6)} %add.99, f32[]{:T(128)} %get-tuple-element.29), channel_id=1, replica_groups=mesh['tm'=8,'bat'=4] {'tm','bat'}, use_global_device_ids=true, to_apply=%region_4.5 | all-reduce | flops 2 | bytes 16 | tf_op jit(solution)/shard_map/psum | solution.py:113
  96.4 0.6 add_reduce_fusion.1
  97.0 1.3 collective-permute-start.3
  98.3 0.8 collective-permute-done.3
  99.1 0.6 multiply_reduce_fusion.1
  99.7 0.3 convolution_bitcast_fusion.2
  100.0 1.9 convolution_bitcast_fusion.12
  102.0 0.2 fusion.8
  102.2 16.9 %all-reduce.1 = f32[16,768]{1,0:T(8,128)S(1)} all-reduce(f32[16,768]{1,0:T(8,128)S(1)} %bitcast.159), channel_id=3, replica_groups=mesh['tm'=8,'bat'=4] {'bat'}, use_global_device_ids=true, to_apply=%region_8.9.clone | all-reduce | flops 12288 | bytes 98304
  119.1 0.6 multiply_reduce_fusion.4
  119.7 7.8 %all-gather.2 = f32[4,4,768]{2,1,0:T(4,128)S(1)} all-gather(f32[1,4,768]{2,1,0:T(4,128)S(1)} %bitcast.162), channel_id=1, replica_groups=mesh['tm'=8,'bat'=4] {'bat'}, dimensions={0}, use_global_device_ids=true | all-gather | bytes 61440 | tf_op jit(solution)/shard_map/all_gather | solution.py:75
  127.6 0.3 convolution_bitcast_fusion.5
  127.9 1.1 convolution_bitcast_fusion.11
  129.0 1.3 collective-permute-start.4
  130.3 0.2 fusion.6
  131.8 43.0 %all-reduce.5 = (f32[]{:T(128)}, f32[]{:T(128)}) all-reduce(f32[]{:T(128)S(6)} %add.106, f32[]{:T(128)} %get-tuple-element.21), channel_id=1, replica_groups=mesh['tm'=8,'bat'=4] {'tm','bat'}, use_global_device_ids=true, to_apply=%region_10.11 | all-reduce | flops 2 | bytes 16 | tf_op jit(solution)/shard_map/psum | solution.py:113
  176.3 0.6 add_reduce_fusion
  176.9 1.5 collective-permute-start.5
  178.4 0.6 collective-permute-done.5
  179.0 0.6 multiply_reduce_fusion
  179.7 0.3 convolution_bitcast_fusion.1
  180.0 1.9 convolution_bitcast_fusion.10
  181.9 0.2 fusion.4
  182.2 17.1 %all-reduce.2 = f32[16,768]{1,0:T(8,128)S(1)} all-reduce(f32[16,768]{1,0:T(8,128)S(1)} %bitcast.160), channel_id=4, replica_groups=mesh['tm'=8,'bat'=4] {'bat'}, use_global_device_ids=true, to_apply=%region_14.15.clone | all-reduce | flops 12288 | bytes 98304
  199.3 0.6 fusion.103
  199.9 7.9 %all-gather.3 = f32[4,4,768]{2,1,0:T(4,128)S(1)} all-gather(f32[1,4,768]{2,1,0:T(4,128)S(1)} %get-tuple-element.37), channel_id=1, replica_groups=mesh['tm'=8,'bat'=4] {'bat'}, dimensions={0}, use_global_device_ids=true | all-gather | bytes 61440 | tf_op jit(solution)/shard_map/all_gather | solution.py:75
  207.8 0.3 convolution_bitcast_fusion.4
  208.2 1.3 collective-permute-start.6
  209.5 1.1 convolution_bitcast_fusion.9
  211.9 41.4 %all-reduce.4 = (f32[]{:T(128)}, f32[]{:T(128)}) all-reduce(f32[]{:T(128)S(6)} %add.113, f32[]{:T(128)} %get-tuple-element.15), channel_id=1, replica_groups=mesh['tm'=8,'bat'=4] {'tm','bat'}, use_global_device_ids=true, to_apply=%region_16.17 | all-reduce | flops 2 | bytes 16 | tf_op jit(solution)/shard_map/psum | solution.py:113
  254.8 0.6 multiply_subtract_fusion.1
  255.4 1.3 collective-permute-start.7
  256.7 0.2 fusion.2
  256.9 0.6 collective-permute-done.7
  257.5 0.6 fusion.71
  258.2 0.3 convolution_bitcast_fusion
  258.5 1.9 convolution_bitcast_fusion.8
  260.4 0.2 fusion
  260.6 17.2 %all-reduce.3 = f32[16,768]{1,0:T(8,128)S(1)} all-reduce(f32[16,768]{1,0:T(8,128)S(1)} %bitcast.161), channel_id=5, replica_groups=mesh['tm'=8,'bat'=4] {'bat'}, use_global_device_ids=true, to_apply=%region_19.20.clone | all-reduce | flops 12288 | bytes 98304
  277.9 0.6 fusion.74
  (55 shorter events, 0.3 us)
Async XLA Ops:
  0.6 14.5 %copy-start = (f32[18,128,128]{2,1,0:T(8,128)S(1)}, f32[18,128,128]{2,1,0:T(8,128)}, u32[]{:S(2)}) copy-start(f32[18,128,128]{2,1,0:T(8,128)} %param.21) | copy-start | bytes 3538948
  0.6 15.8 %copy-start.3 = (f32[16,384]{1,0:T(8,128)S(1)}, f32[16,384]{1,0:T(8,128)}, u32[]{:S(2)}) copy-start(f32[16,384]{1,0:T(8,128)} %param.14) | copy-start | bytes 73732
  0.7 15.8 %copy-start.7 = (f32[384]{0:T(512)S(1)}, f32[384]{0:T(512)}, u32[]{:S(2)}) copy-start(f32[384]{0:T(512)} %param.18) | copy-start | bytes 4612
  0.7 15.8 %copy-start.4 = (f32[16,384]{1,0:T(8,128)S(1)}, f32[16,384]{1,0:T(8,128)}, u32[]{:S(2)}) copy-start(f32[16,384]{1,0:T(8,128)} %param.12) | copy-start | bytes 73732
  0.7 15.8 %copy-start.5 = (f32[16,384]{1,0:T(8,128)S(1)}, f32[16,384]{1,0:T(8,128)}, u32[]{:S(2)}) copy-start(f32[16,384]{1,0:T(8,128)} %param.13) | copy-start | bytes 73732
  0.7 15.8 %copy-start.2 = (f32[16,384]{1,0:T(8,128)S(1)}, f32[16,384]{1,0:T(8,128)}, u32[]{:S(2)}) copy-start(f32[16,384]{1,0:T(8,128)} %param.16) | copy-start | bytes 73732
  0.7 15.8 %copy-start.9 = (f32[384]{0:T(512)S(1)}, f32[384]{0:T(512)}, u32[]{:S(2)}) copy-start(f32[384]{0:T(512)} %param.19) | copy-start | bytes 4612
  1.5 15.0 %collective-permute-start = (f32[1,384]{1,0:T(1,128)S(1)}, f32[1,384]{1,0:T(1,128)S(1)}, u32[]{:S(2)}, u32[]{:S(2)}) collective-permute-start(f32[1,384]{1,0:T(1,128)S(1)} %slice.53), channel_id=1, source_target_pairs={{4,0},{8,4},{12,8},{16,12},{20,16},{24,20},{28,24},{5,1},{9,5},{13... | collective-permute-start | bytes 4616 | tf_op jit(solution)/shard_map/ppermute | solution.py:17
  14.8 3.7 %copy-start.10 = (u32[32]{0:T(128)S(1)}, u32[32]{0:T(128)}, u32[]{:S(2)}) copy-start(u32[32]{0:T(128)} %constant.24) | copy-start | bytes 388
  14.8 5.0 %copy-start.1 = (f32[16,384]{1,0:T(8,128)S(1)}, f32[16,384]{1,0:T(8,128)}, u32[]{:S(2)}) copy-start(f32[16,384]{1,0:T(8,128)} %param.17) | copy-start | bytes 73732
  17.2 2.6 collective-permute-start.1
  19.8 18.9 %copy-start.6 = (f32[768]{0:T(1024)S(1)}, f32[768]{0:T(1024)}, u32[]{:S(2)}) copy-start(f32[768]{0:T(1024)} %param.20) | copy-start | bytes 9220
  19.8 18.9 %copy-start.8 = (f32[4,768]{1,0:T(4,128)S(1)}, f32[4,768]{1,0:T(4,128)}, u32[]{:S(2)}) copy-start(f32[4,768]{1,0:T(4,128)} %param.15) | copy-start | bytes 36868
  48.8 47.6 %collective-permute-start.2 = (f32[1,384]{1,0:T(1,128)S(1)}, f32[1,384]{1,0:T(1,128)S(1)}, u32[]{:S(2)}, u32[]{:S(2)}) collective-permute-start(f32[1,384]{1,0:T(1,128)S(1)} %slice.71), channel_id=1, source_target_pairs={{4,0},{8,4},{12,8},{16,12},{20,16},{24,20},{28,24},{5,1},{9,5},{13... | collective-permute-start | bytes 4616 | tf_op jit(solution)/shard_map/ppermute | solution.py:17
  97.0 2.1 collective-permute-start.3
  129.0 47.3 %collective-permute-start.4 = (f32[1,384]{1,0:T(1,128)S(1)}, f32[1,384]{1,0:T(1,128)S(1)}, u32[]{:S(2)}, u32[]{:S(2)}) collective-permute-start(f32[1,384]{1,0:T(1,128)S(1)} %slice.75), channel_id=1, source_target_pairs={{4,0},{8,4},{12,8},{16,12},{20,16},{24,20},{28,24},{5,1},{9,5},{13... | collective-permute-start | bytes 4616 | tf_op jit(solution)/shard_map/ppermute | solution.py:17
  176.9 2.1 collective-permute-start.5
  208.2 46.6 %collective-permute-start.6 = (f32[1,384]{1,0:T(1,128)S(1)}, f32[1,384]{1,0:T(1,128)S(1)}, u32[]{:S(2)}, u32[]{:S(2)}) collective-permute-start(f32[1,384]{1,0:T(1,128)S(1)} %slice.79), channel_id=1, source_target_pairs={{4,0},{8,4},{12,8},{16,12},{20,16},{24,20},{28,24},{5,1},{9,5},{13... | collective-permute-start | bytes 4616 | tf_op jit(solution)/shard_map/ppermute | solution.py:17
  255.4 2.1 collective-permute-start.7
where the time goes:
time: 281 us; the launch traced here: 278 us
  blocking collectives  228 us (81%)
  matrix products  16.2 us (6%)
  starting transfers between devices  10.5 us (4%)
  between operations  10.1 us (4%)
  other arithmetic  8.92 us (3%)
    psum x3, blocking collectives, shards(): dual_sq = lax.psum(dual_local, ('tm', 'bat'))  128 us
    unnamed x4, blocking collectives  66.9 us
    all_gather x4, blocking collectives, couple_backward(): lax.all_gather(duals, 'bat', axis=0, tiled=True)  33.6 us
    ppermute x8, starting transfers between devices, shifted(): return lax.ppermute(block, axis, route)  10.5 us
    dot_general x4, matrix products, feeder_apply(): jnp.einsum('rjk,jmk->rjm', picked, block_values, precision=HIGH)  7.69 us
  transfers between devices with their start and end apart: 8, of which 3 were waited for; matrix products, arithmetic and copies ran while one was open for 2% of the time, Pallas kernels for 0%

commit v1 on v0

v1 whole, which is shorter than its diff:
```python
import functools

import jax
import jax.numpy as jnp
from jax import lax
from jax.experimental import pallas as pl
from jax.experimental.pallas import tpu as pltpu
from jax.sharding import PartitionSpec as P

ITERS = 4
ETA_STEP = 0.4
EPS_NORM = 1e-06
MESH = pl.DeviceIdType.MESH
F32, BF16 = jnp.float32, jnp.bfloat16


def split(x):
    high = x.astype(BF16)
    return high, (x - high.astype(F32)).astype(BF16)


def stacked(x, axis):
    return jnp.concatenate(split(x), axis=axis)


def quadrants(out, rows, blk):
    return out[:rows, :blk] + (out[rows:, :blk] + out[:rows, blk:])


def kernel(
    tm_n, bat_n,
    power_ref, charge_ref, dyn_ref, feed_ref, price_ref, inflow_ref,
    limit_ref, capacity_ref, feed_limit_ref, values_ref, cols_ref, offsets_ref,
    power_out, charge_out, dyn_out, feed_out,
    feed_all, bars, bar_parts, feed_parts, running, by_rows, by_cols,
    sums, row_next, row_prev, row_charge, own_first, own_last, own_charge, feed_own,
    feed_send, feed_recv, bar_send, bar_recv, sum_send, sum_recv, edge_send, edge_recv,
):
    me_t, me_b = lax.axis_index("tm"), lax.axis_index("bat")
    rows, cols = power_ref.shape
    stored, blk, _ = values_ref.shape
    own = cols // blk
    feed_blocks = feed_ref.shape[1] // blk
    feed_rows = feed_ref.shape[0]
    tiles = rows // 8
    group = own * tiles + 1

    def bat_at(d):
        return (me_t, lax.rem(me_b + d, bat_n))

    def tm_at(d):
        return (lax.rem(me_t + d, tm_n), me_b)

    barrier = pltpu.get_barrier_semaphore()
    for d in range(1, bat_n):
        pl.semaphore_signal(barrier, inc=1, device_id=bat_at(d), device_id_type=MESH)
    for d in range(1, tm_n):
        pl.semaphore_signal(barrier, inc=1, device_id=tm_at(d), device_id_type=MESH)
    pl.semaphore_wait(barrier, bat_n + tm_n - 2)

    started = []

    def send(src, dst, send_sem, recv_sem, device):
        copy = pltpu.make_async_remote_copy(
            src_ref=src, dst_ref=dst, send_sem=send_sem, recv_sem=recv_sem,
            device_id=device, device_id_type=MESH,
        )
        copy.start()
        started.append(copy)
        return copy

    def part(ref, k):
        return ref[:, k * blk:(k + 1) * blk]

    feed_copies = [
        send(feed_ref, feed_all.at[me_b], feed_send.at[d - 1], feed_recv.at[d - 1], bat_at(d))
        for d in range(1, bat_n)
    ]
    own_first[0] = dyn_ref[0:1, :]
    own_last[0] = dyn_ref[rows - 1:rows, :]
    own_charge[...] = charge_ref[rows - 1:rows, :]

    def send_edges(step):
        return [
            send(own_first.at[step], row_next.at[step],
                 edge_send.at[2 * step], edge_recv.at[2 * step], tm_at(tm_n - 1)),
            send(own_last.at[step], row_prev.at[step],
                 edge_send.at[2 * step + 1], edge_recv.at[2 * step + 1], tm_at(1)),
        ]

    edge_copies = send_edges(0) + [
        send(own_charge, row_charge, edge_send.at[2 * ITERS], edge_recv.at[2 * ITERS], tm_at(1))
    ]

    feed_all[me_b] = feed_ref[...]
    for j in range(stored):
        high, low = split(values_ref[j])
        by_cols[j, :, :blk] = high
        by_cols[j, :, blk:] = low
        by_rows[j, :blk, :] = high
        by_rows[j, blk:, :] = low

    row_of = [
        sum((j >= offsets_ref[f]).astype(jnp.int32) for f in range(1, feed_blocks))
        for j in range(stored)
    ]
    col_of = [cols_ref[j] for j in range(stored)]
    inside = [
        [(col_of[j] == me_b * own + k).astype(F32) for k in range(own)] for j in range(stored)
    ]

    def battery_of(feed):
        for f in range(feed_blocks):
            feed_parts[f] = stacked(feed[f], 0)
        total = [jnp.zeros((rows, blk), F32) for _ in range(own)]
        for j in range(stored):
            out = jnp.dot(feed_parts[row_of[j]], by_cols[j], preferred_element_type=F32)
            out = quadrants(out, rows, blk)
            for k in range(own):
                total[k] = total[k] + inside[j][k] * out
        return total

    def feeder_of():
        total = jnp.zeros((rows, blk), F32)
        running[0] = total
        for j in range(stored):
            out = lax.dot_general(
                bar_parts[col_of[j]], by_rows[j], (((1,), (1,)), ((), ())),
                preferred_element_type=F32,
            )
            total = total + quadrants(out, rows, blk)
            running[j + 1] = total
        return [running[offsets_ref[f + 1]] - running[offsets_ref[f]] for f in range(feed_blocks)]

    for copy in feed_copies:
        copy.wait_recv()
    feed = [
        jnp.concatenate([feed_all[n, :, f * blk:(f + 1) * blk] for n in range(bat_n)], axis=0)
        for f in range(feed_blocks)
    ]
    pushed = battery_of(feed)

    for copy in edge_copies:
        copy.wait_recv()

    index = lax.broadcasted_iota(jnp.int32, (rows, blk), 0)
    not_first = jnp.where(me_t == 0, 0.0, 1.0)
    not_last = jnp.where(me_t == tm_n - 1, 0.0, 1.0)
    power = [part(power_ref, k) for k in range(own)]
    charge = [part(charge_ref, k) for k in range(own)]
    dyn = [part(dyn_ref, k) for k in range(own)]
    before = [part(row_charge, k) for k in range(own)]
    weight = jnp.ones((1, blk), F32)

    for step in range(ITERS):
        last = step + 1 == ITERS
        step_primal = ETA_STEP / weight
        step_dual = ETA_STEP * weight
        primal = jnp.zeros((rows, blk), F32)
        moved = jnp.zeros((rows, blk), F32)
        power_new, charge_new, dyn_new, before_new = [], [], [], []
        for k in range(own):
            limit, capacity = part(limit_ref, k), part(capacity_ref, k)
            here = dyn[k]
            following = row_next[step, :, k * blk:(k + 1) * blk] * not_last
            preceding = row_prev[step, :, k * blk:(k + 1) * blk]
            later = jnp.where(index == rows - 1, following, pltpu.roll(here, rows - 1, 0))
            p = power[k] - step_primal * (part(price_ref, k) - here + pushed[k])
            p = jnp.minimum(jnp.maximum(p, -limit), limit)
            c = charge[k] - step_primal * (here - later)
            c = jnp.minimum(jnp.maximum(c, 0.0), capacity)
            b = before[k] - step_primal * (preceding - here[0:1])
            b = jnp.minimum(jnp.maximum(b, 0.0), capacity)
            power_bar = 2.0 * p - power[k]
            charge_bar = 2.0 * c - charge[k]
            before_bar = (2.0 * b - before[k]) * not_first
            earlier = jnp.where(index == 0, before_bar, pltpu.roll(charge_bar, 1, 0))
            n = here + step_dual * (charge_bar - earlier - power_bar - part(inflow_ref, k))
            bars[step, pl.ds(me_b * group + k * tiles, tiles)] = power_bar.reshape(tiles, 8, blk)
            if not last:
                primal = primal + ((p - power[k]) * (p - power[k]) + (c - charge[k]) * (c - charge[k]))
                moved = moved + (n - here) * (n - here)
            power_new.append(p)
            charge_new.append(c)
            dyn_new.append(n)
            before_new.append(b)
        spare = jnp.zeros((6, blk), F32)
        bars[step, me_b * group + own * tiles] = jnp.concatenate(
            [jnp.sum(primal, axis=0, keepdims=True), jnp.sum(moved, axis=0, keepdims=True), spare], axis=0
        )
        mine = bars.at[step, pl.ds(me_b * group, group)]
        bar_copies = [
            send(mine, mine, bar_send.at[step, d - 1], bar_recv.at[step, d - 1], bat_at(d))
            for d in range(1, bat_n)
        ]
        if not last:
            for k in range(own):
                own_first[step + 1, :, k * blk:(k + 1) * blk] = dyn_new[k][0:1]
                own_last[step + 1, :, k * blk:(k + 1) * blk] = dyn_new[k][rows - 1:rows]
            edge_copies = send_edges(step + 1)
        else:
            for k in range(own):
                power_out[:, k * blk:(k + 1) * blk] = power_new[k]
                charge_out[:, k * blk:(k + 1) * blk] = charge_new[k]
                dyn_out[:, k * blk:(k + 1) * blk] = dyn_new[k]
        for copy in bar_copies:
            copy.wait_recv()
        for n in range(bat_n):
            for k in range(own):
                start = n * group + k * tiles
                bar_parts[n * own + k] = stacked(
                    bars[step, start:start + tiles].reshape(rows, blk), 0
                )
        coupled = feeder_of()
        feed_new = [
            jnp.maximum(0.0, feed[f] + step_dual * (coupled[f] - part(feed_limit_ref, f)))
            for f in range(feed_blocks)
        ]
        if not last:
            change = jnp.zeros((rows, blk), F32)
            for f in range(feed_blocks):
                change = change + (feed_new[f] - feed[f]) * (feed_new[f] - feed[f])
            change = jnp.sum(change, axis=0, keepdims=True)
            gathered = bars[step, group - 1]
            for n in range(1, bat_n):
                gathered = gathered + bars[step, n * group + group - 1]
            sums[step, me_t] = jnp.concatenate([gathered[0:1], gathered[1:2] + change], axis=0)
            total = sums.at[step, me_t]
            sum_copies = [
                send(total, total, sum_send.at[step, d - 1], sum_recv.at[step, d - 1], tm_at(d))
                for d in range(1, tm_n)
            ]
            pushed = battery_of(feed_new)
            for copy in sum_copies + edge_copies:
                copy.wait_recv()
            both = sums[step, 0]
            for t in range(1, tm_n):
                both = both + sums[step, t]
            both = jnp.sum(both, axis=1, keepdims=True) + EPS_NORM
            ratio = jnp.sqrt(jnp.broadcast_to(both[1:2], (1, blk)) / jnp.broadcast_to(both[0:1], (1, blk)))
            weight = jnp.sqrt(weight * ratio)
        power, charge, dyn, before, feed = power_new, charge_new, dyn_new, before_new, feed_new

    for n in range(bat_n):
        for f in range(feed_blocks):
            feed_own[n, :, f * blk:(f + 1) * blk] = feed[f][n * feed_rows:(n + 1) * feed_rows]
    feed_out[...] = feed_own[me_b]
    for copy in started:
        copy.wait_send()


def shards(
    tm_n, bat_n, power0, charge0, dyn_dual0, feeder_dual0, price, inflow,
    power_limit, capacity, feeder_limit, block_values, block_cols, block_offsets,
):
    rows, cols = power0.shape
    stored, blk, _ = block_values.shape
    feed_rows, feed_cols = feeder_dual0.shape
    own, feed_blocks = cols // blk, feed_cols // blk
    group = own * (rows // 8) + 1
    vmem = pl.BlockSpec(memory_space=pltpu.VMEM)
    smem = pl.BlockSpec(memory_space=pltpu.SMEM)
    dma = pltpu.SemaphoreType.DMA
    state = jax.ShapeDtypeStruct((rows, cols), F32)
    return pl.pallas_call(
        functools.partial(kernel, tm_n, bat_n),
        out_shape=(state, state, state, jax.ShapeDtypeStruct((feed_rows, feed_cols), F32)),
        in_specs=[vmem] * 10 + [smem] * 2,
        out_specs=(vmem,) * 4,
        scratch_shapes=[
            pltpu.VMEM((bat_n, feed_rows, feed_cols), F32),
            pltpu.VMEM((ITERS, bat_n * group, 8, blk), F32),
            pltpu.VMEM((bat_n * own, 2 * rows, blk), BF16),
            pltpu.VMEM((feed_blocks, 2 * rows, blk), BF16),
            pltpu.VMEM((stored + 1, rows, blk), F32),
            pltpu.VMEM((stored, 2 * blk, blk), BF16),
            pltpu.VMEM((stored, blk, 2 * blk), BF16),
            pltpu.VMEM((ITERS - 1, tm_n, 2, blk), F32),
            pltpu.VMEM((ITERS, 1, cols), F32),
            pltpu.VMEM((ITERS, 1, cols), F32),
            pltpu.VMEM((1, cols), F32),
            pltpu.VMEM((ITERS, 1, cols), F32),
            pltpu.VMEM((ITERS, 1, cols), F32),
            pltpu.VMEM((1, cols), F32),
            pltpu.VMEM((bat_n, feed_rows, feed_cols), F32),
            dma((bat_n - 1,)), dma((bat_n - 1,)),
            dma((ITERS, bat_n - 1)), dma((ITERS, bat_n - 1)),
            dma((ITERS - 1, tm_n - 1)), dma((ITERS - 1, tm_n - 1)),
            dma((2 * ITERS + 1,)), dma((2 * ITERS + 1,)),
        ],
        compiler_params=pltpu.CompilerParams(
            collective_id=0, has_side_effects=True, vmem_limit_bytes=48 * 1024 * 1024
        ),
    )(
        power0, charge0, dyn_dual0, feeder_dual0, price, inflow,
        power_limit.reshape(1, -1), capacity.reshape(1, -1), feeder_limit.reshape(1, -1),
        block_values, block_cols, block_offsets,
    )


def solution(mesh):
    state = P("tm", "bat")
    duals = P(("tm", "bat"), None)
    return jax.shard_map(
        functools.partial(shards, mesh.shape["tm"], mesh.shape["bat"]),
        mesh=mesh,
        in_specs=(state, state, state, duals, state, state, P("bat"), P("bat"), P(), P(), P(), P()),
        out_specs=(state, state, state, duals),
        check_vma=False,
    )
```

time: 281 us -> 49.9 us (0.18)
  blocking collectives: 228 us -> 0 us
  Pallas kernels: 0 us -> 37.2 us
  matrix products: 16.2 us -> 0 us
  starting transfers between devices: 10.5 us -> 0 us
  between operations: 10.1 us -> 0.65 us
  local copies, waits for them, and re-layouts: 2.4 us -> 11.5 us
  other arithmetic: 8.92 us -> 0 us
    psum x3 -> x0, blocking collectives: 128 us -> none  [shards(): dual_sq = lax.psum(dual_local, ('tm', 'bat'))]
    unnamed x4 -> x0, blocking collectives: 66.9 us -> none
    pallas_call x0 -> x1, Pallas kernels: none -> 37.2 us  [shards(): pl.pallas_call(functools.partial(kernel, tm_n, bat_n), out_shape=(state,...]
    all_gather x4 -> x0, blocking collectives: 33.6 us -> none  [couple_backward(): lax.all_gather(duals, 'bat', axis=0, tiled=True)]
    dot_general x24 -> x0, matrix products: 16.2 us -> none  [the longest x4 7.69 us: feeder_apply(): jnp.einsum('rjk,jmk->rjm', picked, block_values, precision=HIGH)]
    ppermute x8 -> x0, starting transfers between devices: 10.5 us -> none  [shifted(): return lax.ppermute(block, axis, route)]
    unnamed x27 -> x22, local copies, waits for them, and re-layouts: 0.69 us -> 9.39 us
    reduce_sum x9 -> x0, other arithmetic: 5.06 us -> none  [the longest x5 3.09 us: shards(): dual_local = jnp.sum(move_dyn * move_dyn) + jnp.sum(move_feed * move_feed)]
  transfers between devices with their start and end apart: 8 -> 0, of which waited for: 3 -> 0; matrix products, arithmetic and copies ran while one was open for 2% -> 0% of each run, Pallas kernels for 0% -> 0%
where the time goes in v1:
time: 49.9 us; the launch traced here: 49.3 us
  Pallas kernels  37.2 us (75%)
  local copies, waits for them, and re-layouts  11.5 us (23%)
  between operations  0.65 us (1%)
    pallas_call x1, Pallas kernels, shards(): pl.pallas_call(functools.partial(kernel, tm_n, bat_n), out_shape=(state,...  37.2 us
    unnamed x22, local copies, waits for them, and re-layouts  9.39 us

profile of v1, /device:TPU:0, one launch (start us, length us, event | category | flops | bytes accessed | tf_op | source)
XLA Modules:
  0.0 49.3 jit_solution(9919668267207537000)
XLA Ops:
  0.6 0.7 %reshape.17.limit_ref = f32[1,384]{1,0:T(1,128)S(1)} reshape(f32[384]{0:T(512)} %param.18) | data formatting | bytes 3072 | tf_op jit(solution)/shard_map/reshape | solution.py:296
  1.3 0.7 %reshape.18.capacity_ref = f32[1,384]{1,0:T(1,128)S(1)} reshape(f32[384]{0:T(512)} %param.19) | data formatting | bytes 3072 | tf_op jit(solution)/shard_map/reshape | solution.py:296
  2.0 0.7 %reshape.19.feed_limit_ref = f32[1,768]{1,0:T(1,128)S(1)} reshape(f32[768]{0:T(1024)} %param.20) | data formatting | bytes 6144 | tf_op jit(solution)/shard_map/reshape | solution.py:296
  2.7 0.0 copy-start
  2.7 1.3 %copy-done = f32[18,128,128]{2,1,0:T(8,128)S(1)} copy-done((f32[18,128,128]{2,1,0:T(8,128)S(1)}, f32[18,128,128]{2,1,0:T(8,128)}, u32[]{:S(2)}) %copy-start) | copy-done | bytes 1179672
  4.0 0.0 copy-start.1
  4.0 0.7 %copy-done.1 = f32[16,384]{1,0:T(8,128)S(1)} copy-done((f32[16,384]{1,0:T(8,128)S(1)}, f32[16,384]{1,0:T(8,128)}, u32[]{:S(2)}) %copy-start.1) | copy-done | bytes 24600
  4.7 0.0 copy-start.2
  4.7 0.7 %copy-done.2 = f32[16,384]{1,0:T(8,128)S(1)} copy-done((f32[16,384]{1,0:T(8,128)S(1)}, f32[16,384]{1,0:T(8,128)}, u32[]{:S(2)}) %copy-start.2) | copy-done | bytes 24600
  5.4 0.0 copy-start.3
  5.4 0.7 %copy-done.3 = f32[16,384]{1,0:T(8,128)S(1)} copy-done((f32[16,384]{1,0:T(8,128)S(1)}, f32[16,384]{1,0:T(8,128)}, u32[]{:S(2)}) %copy-start.3) | copy-done | bytes 24600
  6.2 0.0 copy-start.4
  6.2 0.7 %copy-done.4 = f32[16,384]{1,0:T(8,128)S(1)} copy-done((f32[16,384]{1,0:T(8,128)S(1)}, f32[16,384]{1,0:T(8,128)}, u32[]{:S(2)}) %copy-start.4) | copy-done | bytes 24600
  6.9 0.0 copy-start.5
  6.9 0.7 %copy-done.5 = f32[16,384]{1,0:T(8,128)S(1)} copy-done((f32[16,384]{1,0:T(8,128)S(1)}, f32[16,384]{1,0:T(8,128)}, u32[]{:S(2)}) %copy-start.5) | copy-done | bytes 24600
  7.6 0.0 copy-start.6
  7.7 0.7 %copy-done.6 = f32[4,768]{1,0:T(4,128)S(1)} copy-done((f32[4,768]{1,0:T(4,128)S(1)}, f32[4,768]{1,0:T(4,128)}, u32[]{:S(2)}) %copy-start.6) | copy-done | bytes 12312
  8.4 0.0 copy-start.7
  8.4 0.7 %copy-done.7 = s32[18]{0:T(128)S(1)} copy-done((s32[18]{0:T(128)S(1)}, s32[18]{0:T(128)}, u32[]{:S(2)}) %copy-start.7) | copy-done | bytes 96
  9.0 0.0 copy-start.8
  9.0 0.7 %copy-done.8 = s32[7]{0:T(128)S(1)} copy-done((s32[7]{0:T(128)S(1)}, s32[7]{0:T(128)}, u32[]{:S(2)}) %copy-start.8) | copy-done | bytes 52
  9.7 37.2 %shard_map.147 = (f32[16,384]{1,0:T(8,128)S(1)}, f32[16,384]{1,0:T(8,128)S(1)}, f32[16,384]{1,0:T(8,128)S(1)}, f32[4,768]{1,0:T(4,128)S(1)}) custom-call(f32[16,384]{1,0:T(8,128)S(1)} %copy-done.1, f32[16,384]{1,0:T(8,128)S(1)} %copy-done.2, f32[16,384]{1,0:T(8,128)S(1)} %copy-done.3, f32[4,768]{1,0:T(4,128)S(1)} %copy-done.6, f32[16,384]{1,0:T(8,128)S(1)} %copy-done.4, ...), custom_call_target="tpu_custom_call" | custom-call | tf_op jit(solution)/shard_map/pallas_call | solution.py:265
  46.8 0.6 %copy.20 = f32[16,384]{1,0:T(8,128)} copy(f32[16,384]{1,0:T(8,128)S(1)} %get-tuple-element.8) | data formatting | bytes 49152
  47.5 0.6 %copy.21 = f32[16,384]{1,0:T(8,128)} copy(f32[16,384]{1,0:T(8,128)S(1)} %get-tuple-element.9) | data formatting | bytes 49152
  48.1 0.6 %copy.22 = f32[16,384]{1,0:T(8,128)} copy(f32[16,384]{1,0:T(8,128)S(1)} %get-tuple-element.10) | data formatting | bytes 49152
  48.7 0.6 %copy.23 = f32[4,768]{1,0:T(4,128)} copy(f32[4,768]{1,0:T(4,128)S(1)} %get-tuple-element.11) | data formatting | bytes 24576
Async XLA Ops:
  2.7 1.3 %copy-start = (f32[18,128,128]{2,1,0:T(8,128)S(1)}, f32[18,128,128]{2,1,0:T(8,128)}, u32[]{:S(2)}) copy-start(f32[18,128,128]{2,1,0:T(8,128)} %values_ref.1) | copy-start | bytes 3538948
  4.0 0.7 %copy-start.1 = (f32[16,384]{1,0:T(8,128)S(1)}, f32[16,384]{1,0:T(8,128)}, u32[]{:S(2)}) copy-start(f32[16,384]{1,0:T(8,128)} %power_ref.1) | copy-start | bytes 73732
  4.7 0.7 %copy-start.2 = (f32[16,384]{1,0:T(8,128)S(1)}, f32[16,384]{1,0:T(8,128)}, u32[]{:S(2)}) copy-start(f32[16,384]{1,0:T(8,128)} %charge_ref.1) | copy-start | bytes 73732
  5.4 0.7 %copy-start.3 = (f32[16,384]{1,0:T(8,128)S(1)}, f32[16,384]{1,0:T(8,128)}, u32[]{:S(2)}) copy-start(f32[16,384]{1,0:T(8,128)} %dyn_ref.1) | copy-start | bytes 73732
  6.2 0.7 %copy-start.4 = (f32[16,384]{1,0:T(8,128)S(1)}, f32[16,384]{1,0:T(8,128)}, u32[]{:S(2)}) copy-start(f32[16,384]{1,0:T(8,128)} %price_ref.1) | copy-start | bytes 73732
  6.9 0.7 %copy-start.5 = (f32[16,384]{1,0:T(8,128)S(1)}, f32[16,384]{1,0:T(8,128)}, u32[]{:S(2)}) copy-start(f32[16,384]{1,0:T(8,128)} %inflow_ref.1) | copy-start | bytes 73732
  7.6 0.7 %copy-start.6 = (f32[4,768]{1,0:T(4,128)S(1)}, f32[4,768]{1,0:T(4,128)}, u32[]{:S(2)}) copy-start(f32[4,768]{1,0:T(4,128)} %feed_ref.1) | copy-start | bytes 36868
  8.4 0.7 %copy-start.7 = (s32[18]{0:T(128)S(1)}, s32[18]{0:T(128)}, u32[]{:S(2)}) copy-start(s32[18]{0:T(128)} %cols_ref.1) | copy-start | bytes 220
  9.0 0.7 %copy-start.8 = (s32[7]{0:T(128)S(1)}, s32[7]{0:T(128)}, u32[]{:S(2)}) copy-start(s32[7]{0:T(128)} %offsets_ref.1) | copy-start | bytes 88

commit v2 on v1

--- a/solution.py
+++ b/solution.py
@@ -10,6 +10,7 @@
 ITERS = 4
 ETA_STEP = 0.4
 EPS_NORM = 1e-06
+VMEM_BYTES = 64 * 1024 * 1024
 MESH = pl.DeviceIdType.MESH
 F32, BF16 = jnp.float32, jnp.bfloat16
 
@@ -29,14 +30,25 @@
 
 def kernel(
     tm_n, bat_n,
+    power_in, charge_in, dyn_in, feed_in, price_in, inflow_in,
+    limit_in, capacity_in, feed_limit_in, values_in, cols_in, offsets_in,
+    power_out, charge_out, dyn_out, feed_out,
     power_ref, charge_ref, dyn_ref, feed_ref, price_ref, inflow_ref,
-    limit_ref, capacity_ref, feed_limit_ref, values_ref, cols_ref, offsets_ref,
-    power_out, charge_out, dyn_out, feed_out,
+    limit_ref, capacity_ref, feed_limit_ref, values_ref, cols_ref, offsets_ref, fetch_sem,
     feed_all, bars, bar_parts, feed_parts, running, by_rows, by_cols,
     sums, row_next, row_prev, row_charge, own_first, own_last, own_charge, feed_own,
     feed_send, feed_recv, bar_send, bar_recv, sum_send, sum_recv, edge_send, edge_recv,
 ):
     me_t, me_b = lax.axis_index("tm"), lax.axis_index("bat")
+    pairs = (
+        (feed_in, feed_ref), (dyn_in, dyn_ref), (charge_in, charge_ref), (values_in, values_ref),
+        (cols_in, cols_ref), (offsets_in, offsets_ref), (power_in, power_ref), (price_in, price_ref),
+        (inflow_in, inflow_ref), (limit_in, limit_ref), (capacity_in, capacity_ref),
+        (feed_limit_in, feed_limit_ref),
+    )
+    fetches = [pltpu.make_async_copy(a, b, fetch_sem.at[i]) for i, (a, b) in enumerate(pairs)]
+    for copy in fetches:
+        copy.start()
     rows, cols = power_ref.shape
     stored, blk, _ = values_ref.shape
     own = cols // blk
@@ -72,10 +84,16 @@
     def part(ref, k):
         return ref[:, k * blk:(k + 1) * blk]
 
+    def row_part(ref, k):
+        return ref[k * blk:(k + 1) * blk].reshape(1, blk)
+
+    fetches[0].wait()
     feed_copies = [
         send(feed_ref, feed_all.at[me_b], feed_send.at[d - 1], feed_recv.at[d - 1], bat_at(d))
         for d in range(1, bat_n)
     ]
+    fetches[1].wait()
+    fetches[2].wait()
     own_first[0] = dyn_ref[0:1, :]
     own_last[0] = dyn_ref[rows - 1:rows, :]
     own_charge[...] = charge_ref[rows - 1:rows, :]
@@ -93,6 +111,8 @@
     ]
 
     feed_all[me_b] = feed_ref[...]
+    for copy in fetches[3:]:
+        copy.wait()
     for j in range(stored):
         high, low = split(values_ref[j])
         by_cols[j, :, :blk] = high
@@ -160,7 +180,7 @@
         moved = jnp.zeros((rows, blk), F32)
         power_new, charge_new, dyn_new, before_new = [], [], [], []
         for k in range(own):
-            limit, capacity = part(limit_ref, k), part(capacity_ref, k)
+            limit, capacity = row_part(limit_ref, k), row_part(capacity_ref, k)
             here = dyn[k]
             following = row_next[step, :, k * blk:(k + 1) * blk] * not_last
             preceding = row_prev[step, :, k * blk:(k + 1) * blk]
@@ -213,7 +233,7 @@
                 )
         coupled = feeder_of()
         feed_new = [
-            jnp.maximum(0.0, feed[f] + step_dual * (coupled[f] - part(feed_limit_ref, f)))
+            jnp.maximum(0.0, feed[f] + step_dual * (coupled[f] - row_part(feed_limit_ref, f)))
             for f in range(feed_blocks)
         ]
         if not last:
@@ -249,6 +269,19 @@
         copy.wait_send()
 
 
+def hand_over(*refs):
+    half = (len(refs) - 1) // 2
+    sem = refs[-1]
+    copies = [
+        pltpu.make_async_copy(a, b, sem.at[i])
+        for i, (a, b) in enumerate(zip(refs[:half], refs[half:-1]))
+    ]
+    for copy in copies:
+        copy.start()
+    for copy in copies:
+        copy.wait()
+
+
 def shards(
     tm_n, bat_n, power0, charge0, dyn_dual0, feeder_dual0, price, inflow,
     power_limit, capacity, feeder_limit, block_values, block_cols, block_offsets,
@@ -259,15 +292,23 @@
     own, feed_blocks = cols // blk, feed_cols // blk
     group = own * (rows // 8) + 1
     vmem = pl.BlockSpec(memory_space=pltpu.VMEM)
-    smem = pl.BlockSpec(memory_space=pltpu.SMEM)
     dma = pltpu.SemaphoreType.DMA
     state = jax.ShapeDtypeStruct((rows, cols), F32)
-    return pl.pallas_call(
+    outs = (state, state, state, jax.ShapeDtypeStruct((feed_rows, feed_cols), F32))
+    hbm = pl.BlockSpec(memory_space=pltpu.HBM)
+    operands = (
+        power0, charge0, dyn_dual0, feeder_dual0, price, inflow,
+        power_limit, capacity, feeder_limit, block_values, block_cols, block_offsets,
+    )
+    results = pl.pallas_call(
         functools.partial(kernel, tm_n, bat_n),
-        out_shape=(state, state, state, jax.ShapeDtypeStruct((feed_rows, feed_cols), F32)),
-        in_specs=[vmem] * 10 + [smem] * 2,
+        out_shape=outs,
+        in_specs=[hbm] * len(operands),
         out_specs=(vmem,) * 4,
         scratch_shapes=[
+            *[pltpu.VMEM(x.shape, x.dtype) for x in operands[:10]],
+            *[pltpu.SMEM(x.shape, x.dtype) for x in operands[10:]],
+            dma((len(operands),)),
             pltpu.VMEM((bat_n, feed_rows, feed_cols), F32),
             pltpu.VMEM((ITERS, bat_n * group, 8, blk), F32),
             pltpu.VMEM((bat_n * own, 2 * rows, blk), BF16),
@@ -289,13 +330,17 @@
             dma((2 * ITERS + 1,)), dma((2 * ITERS + 1,)),
         ],
         compiler_params=pltpu.CompilerParams(
-            collective_id=0, has_side_effects=True, vmem_limit_bytes=48 * 1024 * 1024
+            collective_id=0, has_side_effects=True, vmem_limit_bytes=VMEM_BYTES
         ),
-    )(
-        power0, charge0, dyn_dual0, feeder_dual0, price, inflow,
-        power_limit.reshape(1, -1), capacity.reshape(1, -1), feeder_limit.reshape(1, -1),
-        block_values, block_cols, block_offsets,
-    )
+    )(*operands)
+    return pl.pallas_call(
+        hand_over,
+        out_shape=outs,
+        in_specs=[hbm] * 4,
+        out_specs=(hbm,) * 4,
+        scratch_shapes=[dma((4,))],
+        compiler_params=pltpu.CompilerParams(vmem_limit_bytes=VMEM_BYTES),
+    )(*results)
 
 
 def solution(mesh):

time: 49.9 us -> 41.9 us (0.84); the launches traced: 49.3 us -> 41.8 us
  local copies, waits for them, and re-layouts: 11.5 us -> 0 us
  Pallas kernels: 37.2 us -> 41.1 us
    unnamed x22 -> x0, local copies, waits for them, and re-layouts: 9.39 us -> none
    pallas_call x1 -> x2, Pallas kernels: 37.2 us -> 41.1 us  [the longest x1 37.4 us: shards(): pl.pallas_call(functools.partial(kernel, tm_n, bat_n), out_shape=outs, in...]
    reshape x3 -> x0, local copies, waits for them, and re-layouts: 2.06 us -> none  [the longest x1 0.69 us: shards(): feeder_limit.reshape(1, -1)]
where the time goes in v2:
time: 41.9 us; the launch traced here: 41.8 us
  Pallas kernels  41.1 us (98%)
  between operations  0.64 us (2%)
    pallas_call x1, Pallas kernels, shards(): pl.pallas_call(functools.partial(kernel, tm_n, bat_n), out_shape=outs, in...  37.4 us
    pallas_call x1, Pallas kernels, shards(): pl.pallas_call(hand_over, out_shape=outs, in_specs=[hbm] * 4, out_specs=(...  3.75 us

profile of v2, /device:TPU:0, one launch (start us, length us, event | category | flops | bytes accessed | tf_op | source)
XLA Modules:
  0.0 41.8 jit_solution(18074941273776154547)
XLA Ops:
  0.6 37.4 %shard_map.147 = (f32[16,384]{1,0:T(8,128)}, f32[16,384]{1,0:T(8,128)}, f32[16,384]{1,0:T(8,128)}, f32[4,768]{1,0:T(4,128)}) custom-call(f32[16,384]{1,0:T(8,128)} %power_in.1, f32[16,384]{1,0:T(8,128)} %charge_in.1, f32[16,384]{1,0:T(8,128)} %dyn_in.1, f32[4,768]{1,0:T(4,128)} %feed_in.1, f32[16,384]{1,0:T(8,128)} %price_in.1, f32[16,384]{1,0:T(8,128)} %inflow_in.1, ...), custom_call_target="tpu_custom_call" | custom-call | tf_op jit(solution)/shard_map/pallas_call | solution.py:303
  38.0 3.7 %shard_map.148 = (f32[16,384]{1,0:T(8,128)}, f32[16,384]{1,0:T(8,128)}, f32[16,384]{1,0:T(8,128)}, f32[4,768]{1,0:T(4,128)}) custom-call(f32[16,384]{1,0:T(8,128)} %get-tuple-element.8.refs_0_, f32[16,384]{1,0:T(8,128)} %get-tuple-element.9.refs_1_, f32[16,384]{1,0:T(8,128)} %get-tuple-element.10.refs_2_, f32[4,768]{1,0:T(4,128)} %get-tuple-element.11.refs_3_), custom_call_target="tpu_custom_call" | custom-call | tf_op jit(solution)/shard_map/pallas_call | solution.py:336

commit v3 on v2

v3 whole, which is shorter than its diff:
```python
import functools

import jax
import jax.numpy as jnp
from jax import lax
from jax.experimental import pallas as pl
from jax.experimental.pallas import tpu as pltpu
from jax.sharding import PartitionSpec as P

ITERS = 4
ETA_STEP = 0.4
EPS_NORM = 1e-06
VMEM_BYTES = 64 * 1024 * 1024
MESH = pl.DeviceIdType.MESH
F32, BF16 = jnp.float32, jnp.bfloat16


def split(x):
    high = x.astype(BF16)
    return high, (x - high.astype(F32)).astype(BF16)


def stacked(x, axis):
    return jnp.concatenate(split(x), axis=axis)


def quadrants(out, rows, blk):
    return out[:rows, :blk] + (out[rows:, :blk] + out[:rows, blk:])


def kernel(
    tm_n, bat_n,
    power_in, charge_in, dyn_in, feed_in, price_in, inflow_in,
    limit_in, capacity_in, feed_limit_in, values_in, cols_in, offsets_in,
    power_out, charge_out, dyn_out, feed_out,
    power_ref, charge_ref, dyn_ref, feed_ref, price_ref, inflow_ref,
    limit_ref, capacity_ref, feed_limit_ref, values_ref, cols_ref, offsets_ref, fetch_sem,
    feed_all, early, bars, late, bar_parts, feed_parts, running, by_rows, by_cols,
    sums, row_next, row_prev, row_charge, own_first, own_last, own_charge, feed_own, results,
    feed_send, feed_recv, early_send, early_recv, bar_send, bar_recv, late_send, late_recv,
    sum_send, sum_recv, edge_send, edge_recv, cross_send, cross_recv,
):
    me_t, me_b = lax.axis_index("tm"), lax.axis_index("bat")
    pairs = (
        (feed_in, feed_ref), (dyn_in, dyn_ref), (charge_in, charge_ref),
        (power_in, power_ref), (price_in, price_ref), (inflow_in, inflow_ref),
        (limit_in, limit_ref), (capacity_in, capacity_ref),
        (cols_in, cols_ref), (offsets_in, offsets_ref), (feed_limit_in, feed_limit_ref),
        (values_in, values_ref),
    )
    fetches = [pltpu.make_async_copy(a, b, fetch_sem.at[i]) for i, (a, b) in enumerate(pairs)]
    for copy in fetches:
        copy.start()
    rows, cols = power_ref.shape
    stored, blk, _ = values_ref.shape
    own = cols // blk
    blocks = bat_n * own
    feed_blocks = feed_ref.shape[1] // blk
    feed_rows = feed_ref.shape[0]
    base = me_b * own

    def at(t, b):
        return (lax.rem(me_t + t, tm_n), lax.rem(me_b + b, bat_n))

    before_t, after_t = tm_n - 1, 1
    partners = (
        [(0, d) for d in range(1, bat_n)]
        + [(d, 0) for d in range(1, tm_n)]
        + [(t, d) for t in (before_t, after_t) for d in range(1, bat_n)]
    )
    barrier = pltpu.get_barrier_semaphore()
    for t, b in partners:
        pl.semaphore_signal(barrier, inc=1, device_id=at(t, b), device_id_type=MESH)
    pl.semaphore_wait(barrier, len(partners))

    started = []

    def send(src, dst, send_sem, recv_sem, device):
        copy = pltpu.make_async_remote_copy(
            src_ref=src, dst_ref=dst, send_sem=send_sem, recv_sem=recv_sem,
            device_id=device, device_id_type=MESH,
        )
        copy.start()
        started.append(copy)
        return copy

    def spread(ref, send_sems, recv_sems):
        mine = ref.at[pl.ds(base, own)]
        return [
            send(mine, mine, send_sems.at[d - 1], recv_sems.at[d - 1], at(0, d))
            for d in range(1, bat_n)
        ]

    def in_blocks(ref):
        return jnp.stack([ref[:, k * blk:(k + 1) * blk] for k in range(own)], axis=0)

    def row_part(ref, k):
        return ref[k * blk:(k + 1) * blk].reshape(1, blk)

    def row_blocks(ref):
        return jnp.stack([row_part(ref, k) for k in range(own)], axis=0)

    fetches[0].wait()
    feed_copies = [
        send(feed_ref, feed_all.at[me_b], feed_send.at[d - 1], feed_recv.at[d - 1], at(0, d))
        for d in range(1, bat_n)
    ]
    fetches[1].wait()
    fetches[2].wait()
    dyn, charge = in_blocks(dyn_ref), in_blocks(charge_ref)
    mine = pl.ds(base, own)
    own_first[0, mine] = dyn[:, 0:1]
    own_last[0, mine] = dyn[:, rows - 1:rows]
    own_charge[...] = charge[:, rows - 1:rows]

    def send_edges(step, span):
        return [
            send(own_first.at[step, span], row_next.at[step, span],
                 edge_send.at[2 * step], edge_recv.at[2 * step], at(before_t, 0)),
            send(own_last.at[step, span], row_prev.at[step, span],
                 edge_send.at[2 * step + 1], edge_recv.at[2 * step + 1], at(after_t, 0)),
        ]

    edge_copies = send_edges(0, mine) + [
        send(own_charge, row_charge, edge_send.at[2 * ITERS], edge_recv.at[2 * ITERS], at(after_t, 0))
    ]
    for copy in fetches[3:8]:
        copy.wait()
    power, price, inflow = in_blocks(power_ref), in_blocks(price_ref), in_blocks(inflow_ref)
    limit, capacity = row_blocks(limit_ref), row_blocks(capacity_ref)
    early[mine, 0:rows] = price
    early[mine, rows:2 * rows] = inflow
    early[mine, 2 * rows:3 * rows] = power
    early[mine, 3 * rows:3 * rows + 8] = jnp.concatenate(
        [limit, capacity, jnp.zeros((own, 6, blk), F32)], axis=1
    )
    early_copies = spread(early, early_send, early_recv)

    feed_all[me_b] = feed_ref[...]
    for copy in fetches[8:]:
        copy.wait()
    for j in range(stored):
        high, low = split(values_ref[j])
        by_cols[j, :, :blk] = high
        by_cols[j, :, blk:] = low
        by_rows[j, :blk, :] = high
        by_rows[j, blk:, :] = low

    row_of = [
        sum((j >= offsets_ref[f]).astype(jnp.int32) for f in range(1, feed_blocks))
        for j in range(stored)
    ]
    col_of = [cols_ref[j] for j in range(stored)]

    def battery_of(feed, first, count):
        for f in range(feed_blocks):
            feed_parts[f] = stacked(feed[f], 0)
        ids = lax.broadcasted_iota(jnp.int32, (count, rows, blk), 0)
        total = jnp.zeros((count, rows, blk), F32)
        for j in range(stored):
            out = jnp.dot(feed_parts[row_of[j]], by_cols[j], preferred_element_type=F32)
            out = quadrants(out, rows, blk)
            total = total + jnp.where(ids == col_of[j] - first, out[None], 0.0)
        return total

    def feeder_of(bar):
        bar_parts[:, :rows], bar_parts[:, rows:] = split(bar)
        total = jnp.zeros((rows, blk), F32)
        running[0] = total
        for j in range(stored):
            out = lax.dot_general(
                bar_parts[col_of[j]], by_rows[j], (((1,), (1,)), ((), ())),
                preferred_element_type=F32,
            )
            total = total + quadrants(out, rows, blk)
            running[j + 1] = total
        return [running[offsets_ref[f + 1]] - running[offsets_ref[f]] for f in range(feed_blocks)]

    for copy in feed_copies:
        copy.wait_recv()
    feed = [
        jnp.concatenate([feed_all[n, :, f * blk:(f + 1) * blk] for n in range(bat_n)], axis=0)
        for f in range(feed_blocks)
    ]
    pushed = battery_of(feed, base, own)

    for copy in edge_copies:
        copy.wait_recv()

    not_first = jnp.where(me_t == 0, 0.0, 1.0)
    not_last = jnp.where(me_t == tm_n - 1, 0.0, 1.0)
    before = row_charge[...]
    following, preceding = row_next[0, mine], row_prev[0, mine]
    weight = jnp.ones((1, 1, blk), F32)

    for step in range(ITERS):
        last = step + 1 == ITERS
        step_primal = ETA_STEP / weight
        step_dual = ETA_STEP * weight
        index = lax.broadcasted_iota(jnp.int32, power.shape, 1)
        later = jnp.where(index == rows - 1, following * not_last, pltpu.roll(dyn, rows - 1, 1))
        power_new = power - step_primal * (price - dyn + pushed)
        power_new = jnp.minimum(jnp.maximum(power_new, -limit), limit)
        power_bar = 2.0 * power_new - power
        charge_new = charge - step_primal * (dyn - later)
        charge_new = jnp.minimum(jnp.maximum(charge_new, 0.0), capacity)
        before_new = before - step_primal * (preceding - dyn[:, 0:1])
        before_new = jnp.minimum(jnp.maximum(before_new, 0.0), capacity)
        charge_bar = 2.0 * charge_new - charge
        before_bar = (2.0 * before_new - before) * not_first
        earlier = jnp.where(index == 0, before_bar, pltpu.roll(charge_bar, 1, 1))
        dyn_new = dyn + step_dual * (charge_bar - earlier - power_bar - inflow)
        if not last:
            primal = (power_new - power) * (power_new - power) + (charge_new - charge) * (charge_new - charge)
            moved = (dyn_new - dyn) * (dyn_new - dyn)
            first_row, last_row = dyn_new[:, 0:1], dyn_new[:, rows - 1:rows]
        if step == 0:
            bars[mine, 0:rows] = power_bar
            bars[mine, rows:rows + 8] = jnp.concatenate(
                [jnp.sum(primal, axis=1, keepdims=True), jnp.sum(moved, axis=1, keepdims=True),
                 jnp.zeros((own, 6, blk), F32)], axis=1
            )
            bar_copies = spread(bars, bar_send, bar_recv)
            own_first[1, mine] = first_row
            own_last[1, mine] = last_row
            edge_copies = []
            for d in range(bat_n):
                edge_copies += [
                    send(own_first.at[1, mine], row_next.at[1, mine],
                         cross_send.at[0, d], cross_recv.at[0, d], at(before_t, d)),
                    send(own_last.at[1, mine], row_prev.at[1, mine],
                         cross_send.at[1, d], cross_recv.at[1, d], at(after_t, d)),
                ]
            late[mine, 0:rows] = charge_new
            late[mine, rows:2 * rows] = dyn_new
            late[mine, 2 * rows:2 * rows + 8] = jnp.concatenate(
                [before_new, jnp.zeros((own, 7, blk), F32)], axis=1
            )
            late_copies = spread(late, late_send, late_recv)
            for copy in bar_copies:
                copy.wait_recv()
            power_bar = bars[:, 0:rows]
            gathered = jnp.sum(bars[:, rows:rows + 8], axis=0)[0:2]
        elif not last:
            everything = slice(0, blocks)
            own_first[step + 1] = first_row
            own_last[step + 1] = last_row
            edge_copies = send_edges(step + 1, everything)
            gathered = jnp.concatenate(
                [jnp.sum(jnp.sum(primal, axis=0), axis=0, keepdims=True),
                 jnp.sum(jnp.sum(moved, axis=0), axis=0, keepdims=True)], axis=0
            )
        coupled = feeder_of(power_bar)
        flat_dual = step_dual.reshape(1, blk)
        feed_new = [
            jnp.maximum(0.0, feed[f] + flat_dual * (coupled[f] - row_part(feed_limit_ref, f)))
            for f in range(feed_blocks)
        ]
        if not last:
            change = jnp.zeros((rows, blk), F32)
            for f in range(feed_blocks):
                change = change + (feed_new[f] - feed[f]) * (feed_new[f] - feed[f])
            change = jnp.sum(change, axis=0, keepdims=True)
            sums[step, me_t] = jnp.concatenate([gathered[0:1], gathered[1:2] + change], axis=0)
            total = sums.at[step, me_t]
            sum_copies = [
                send(total, total, sum_send.at[step, d - 1], sum_recv.at[step, d - 1], at(d, 0))
                for d in range(1, tm_n)
            ]
            pushed = battery_of(feed_new, 0, blocks)
            if step == 0:
                for copy in early_copies + late_copies:
                    copy.wait_recv()
                price, inflow = early[:, 0:rows], early[:, rows:2 * rows]
                power_new = 0.5 * (power_bar + early[:, 2 * rows:3 * rows])
                limit = early[:, 3 * rows:3 * rows + 1]
                capacity = early[:, 3 * rows + 1:3 * rows + 2]
                charge_new, dyn_new = late[:, 0:rows], late[:, rows:2 * rows]
                before_new = late[:, 2 * rows:2 * rows + 1]
            for copy in edge_copies + sum_copies:
                copy.wait_recv()
            following, preceding = row_next[step + 1], row_prev[step + 1]
            both = sums[step, 0]
            for t in range(1, tm_n):
                both = both + sums[step, t]
            both = jnp.sum(both, axis=1, keepdims=True) + EPS_NORM
            ratio = jnp.sqrt(jnp.broadcast_to(both[1:2], (1, blk)) / jnp.broadcast_to(both[0:1], (1, blk)))
            weight = jnp.sqrt(weight * ratio.reshape(1, 1, blk))
        power, charge, dyn, before, feed = power_new, charge_new, dyn_new, before_new, feed_new
        if step == ITERS - 1:
            for n, value in enumerate((power, charge, dyn)):
                results[n] = value

    for n, out in enumerate((power_out, charge_out, dyn_out)):
        for k in range(own):
            out[:, k * blk:(k + 1) * blk] = results[n, base + k]
    for n in range(bat_n):
        for f in range(feed_blocks):
            feed_own[n, :, f * blk:(f + 1) * blk] = feed[f][n * feed_rows:(n + 1) * feed_rows]
    feed_out[...] = feed_own[me_b]
    for copy in started:
        copy.wait_send()


def hand_over(*refs):
    half = len(refs) // 2
    for source, out in zip(refs[:half], refs[half:]):
        out[...] = source[...]


def shards(
    tm_n, bat_n, power0, charge0, dyn_dual0, feeder_dual0, price, inflow,
    power_limit, capacity, feeder_limit, block_values, block_cols, block_offsets,
):
    rows, cols = power0.shape
    stored, blk, _ = block_values.shape
    feed_rows, feed_cols = feeder_dual0.shape
    own, feed_blocks = cols // blk, feed_cols // blk
    blocks = bat_n * own
    vmem = pl.BlockSpec(memory_space=pltpu.VMEM)
    dma = pltpu.SemaphoreType.DMA
    state = jax.ShapeDtypeStruct((rows, cols), F32)
    outs = (state, state, state, jax.ShapeDtypeStruct((feed_rows, feed_cols), F32))
    hbm = pl.BlockSpec(memory_space=pltpu.HBM)
    operands = (
        power0, charge0, dyn_dual0, feeder_dual0, price, inflow,
        power_limit, capacity, feeder_limit, block_values, block_cols, block_offsets,
    )
    results = pl.pallas_call(
        functools.partial(kernel, tm_n, bat_n),
        out_shape=outs,
        in_specs=[hbm] * len(operands),
        out_specs=(vmem,) * 4,
        scratch_shapes=[
            *[pltpu.VMEM(x.shape, x.dtype) for x in operands[:10]],
            *[pltpu.SMEM(x.shape, x.dtype) for x in operands[10:]],
            dma((len(operands),)),
            pltpu.VMEM((bat_n, feed_rows, feed_cols), F32),
            pltpu.VMEM((blocks, 3 * rows + 8, blk), F32),
            pltpu.VMEM((blocks, rows + 8, blk), F32),
            pltpu.VMEM((blocks, 2 * rows + 8, blk), F32),
            pltpu.VMEM((blocks, 2 * rows, blk), BF16),
            pltpu.VMEM((feed_blocks, 2 * rows, blk), BF16),
            pltpu.VMEM((stored + 1, rows, blk), F32),
            pltpu.VMEM((stored, 2 * blk, blk), BF16),
            pltpu.VMEM((stored, blk, 2 * blk), BF16),
            pltpu.VMEM((ITERS - 1, tm_n, 2, blk), F32),
            pltpu.VMEM((ITERS, blocks, 1, blk), F32),
            pltpu.VMEM((ITERS, blocks, 1, blk), F32),
            pltpu.VMEM((own, 1, blk), F32),
            pltpu.VMEM((ITERS, blocks, 1, blk), F32),
            pltpu.VMEM((ITERS, blocks, 1, blk), F32),
            pltpu.VMEM((own, 1, blk), F32),
            pltpu.VMEM((bat_n, feed_rows, feed_cols), F32),
            pltpu.VMEM((3, blocks, rows, blk), F32),
            *[dma((bat_n - 1,)) for _ in range(8)],
            dma((ITERS - 1, tm_n - 1)), dma((ITERS - 1, tm_n - 1)),
            dma((2 * ITERS + 1,)), dma((2 * ITERS + 1,)),
            dma((2, bat_n)), dma((2, bat_n)),
        ],
        compiler_params=pltpu.CompilerParams(
            collective_id=0, has_side_effects=True, vmem_limit_bytes=VMEM_BYTES
        ),
    )(*operands)
    return pl.pallas_call(
        hand_over,
        out_shape=outs,
        in_specs=[vmem] * 4,
        out_specs=(vmem,) * 4,
        compiler_params=pltpu.CompilerParams(vmem_limit_bytes=VMEM_BYTES),
    )(*results)


def solution(mesh):
    state = P("tm", "bat")
    duals = P(("tm", "bat"), None)
    return jax.shard_map(
        functools.partial(shards, mesh.shape["tm"], mesh.shape["bat"]),
        mesh=mesh,
        in_specs=(state, state, state, duals, state, state, P("bat"), P("bat"), P(), P(), P(), P()),
        out_specs=(state, state, state, duals),
        check_vma=False,
    )
```

time: 41.9 us -> 32 us (0.76)
  Pallas kernels: 41.1 us -> 31.2 us
    pallas_call x1, Pallas kernels: 37.4 us -> 29.8 us  [shards(): pl.pallas_call(functools.partial(kernel, tm_n, bat_n), out_shape=outs, in...]
    pallas_call x1, Pallas kernels: 3.75 us -> 1.41 us  [shards(): pl.pallas_call(hand_over, out_shape=outs, in_specs=[vmem] * 4, out_specs=...]
where the time goes in v3:
time: 32 us; the launch traced here: 31.8 us
  Pallas kernels  31.2 us (98%)
  between operations  0.64 us (2%)
    pallas_call x1, Pallas kernels, shards(): pl.pallas_call(functools.partial(kernel, tm_n, bat_n), out_shape=outs, in...  29.8 us
    pallas_call x1, Pallas kernels, shards(): pl.pallas_call(hand_over, out_shape=outs, in_specs=[vmem] * 4, out_specs=...  1.41 us

profile of v3, /device:TPU:0, one launch (start us, length us, event | category | flops | bytes accessed | tf_op | source)
XLA Modules:
  0.0 31.8 jit_solution(11963162436626138545)
XLA Ops:
  0.6 29.8 %shard_map.147 = (f32[16,384]{1,0:T(8,128)}, f32[16,384]{1,0:T(8,128)}, f32[16,384]{1,0:T(8,128)}, f32[4,768]{1,0:T(4,128)}) custom-call(f32[16,384]{1,0:T(8,128)} %power_in.1, f32[16,384]{1,0:T(8,128)} %charge_in.1, f32[16,384]{1,0:T(8,128)} %dyn_in.1, f32[4,768]{1,0:T(4,128)} %feed_in.1, f32[16,384]{1,0:T(8,128)} %price_in.1, f32[16,384]{1,0:T(8,128)} %inflow_in.1, ...), custom_call_target="tpu_custom_call" | custom-call | tf_op jit(solution)/shard_map/pallas_call | solution.py:329
  30.4 1.4 %shard_map.148 = (f32[16,384]{1,0:T(8,128)}, f32[16,384]{1,0:T(8,128)}, f32[16,384]{1,0:T(8,128)}, f32[4,768]{1,0:T(4,128)}) custom-call(f32[16,384]{1,0:T(8,128)} %get-tuple-element.8.refs_0_, f32[16,384]{1,0:T(8,128)} %get-tuple-element.9.refs_1_, f32[16,384]{1,0:T(8,128)} %get-tuple-element.10.refs_2_, f32[4,768]{1,0:T(4,128)} %get-tuple-element.11.refs_3_), custom_call_target="tpu_custom_call" | custom-call | tf_op jit(solution)/shard_map/pallas_call | solution.py:365

commit v4 on v3

--- a/solution.py
+++ b/solution.py
@@ -71,7 +71,6 @@
     barrier = pltpu.get_barrier_semaphore()
     for t, b in partners:
         pl.semaphore_signal(barrier, inc=1, device_id=at(t, b), device_id_type=MESH)
-    pl.semaphore_wait(barrier, len(partners))
 
     started = []
 
@@ -101,10 +100,6 @@
         return jnp.stack([row_part(ref, k) for k in range(own)], axis=0)
 
     fetches[0].wait()
-    feed_copies = [
-        send(feed_ref, feed_all.at[me_b], feed_send.at[d - 1], feed_recv.at[d - 1], at(0, d))
-        for d in range(1, bat_n)
-    ]
     fetches[1].wait()
     fetches[2].wait()
     dyn, charge = in_blocks(dyn_ref), in_blocks(charge_ref)
@@ -121,9 +116,6 @@
                  edge_send.at[2 * step + 1], edge_recv.at[2 * step + 1], at(after_t, 0)),
         ]
 
-    edge_copies = send_edges(0, mine) + [
-        send(own_charge, row_charge, edge_send.at[2 * ITERS], edge_recv.at[2 * ITERS], at(after_t, 0))
-    ]
     for copy in fetches[3:8]:
         copy.wait()
     power, price, inflow = in_blocks(power_ref), in_blocks(price_ref), in_blocks(inflow_ref)
@@ -134,6 +126,14 @@
     early[mine, 3 * rows:3 * rows + 8] = jnp.concatenate(
         [limit, capacity, jnp.zeros((own, 6, blk), F32)], axis=1
     )
+    pl.semaphore_wait(barrier, len(partners))
+    feed_copies = [
+        send(feed_ref, feed_all.at[me_b], feed_send.at[d - 1], feed_recv.at[d - 1], at(0, d))
+        for d in range(1, bat_n)
+    ]
+    edge_copies = send_edges(0, mine) + [
+        send(own_charge, row_charge, edge_send.at[2 * ITERS], edge_recv.at[2 * ITERS], at(after_t, 0))
+    ]
     early_copies = spread(early, early_send, early_recv)
 
     feed_all[me_b] = feed_ref[...]

time: 32 us -> 32.1 us (level)
  no operation moved by 1% of the time
where the time goes in v4:
time: 32.1 us; the launch traced here: 31.8 us
  Pallas kernels  31.2 us (97%)
  between operations  0.64 us (2%)
    pallas_call x1, Pallas kernels, shards(): pl.pallas_call(functools.partial(kernel, tm_n, bat_n), out_shape=outs, in...  29.8 us
    pallas_call x1, Pallas kernels, shards(): pl.pallas_call(hand_over, out_shape=outs, in_specs=[vmem] * 4, out_specs=...  1.41 us

profile of v4, /device:TPU:0, one launch (start us, length us, event | category | flops | bytes accessed | tf_op | source)
XLA Modules:
  0.0 31.8 jit_solution(11486677044874248637)
XLA Ops:
  0.6 29.8 %shard_map.147 = (f32[16,384]{1,0:T(8,128)}, f32[16,384]{1,0:T(8,128)}, f32[16,384]{1,0:T(8,128)}, f32[4,768]{1,0:T(4,128)}) custom-call(f32[16,384]{1,0:T(8,128)} %power_in.1, f32[16,384]{1,0:T(8,128)} %charge_in.1, f32[16,384]{1,0:T(8,128)} %dyn_in.1, f32[4,768]{1,0:T(4,128)} %feed_in.1, f32[16,384]{1,0:T(8,128)} %price_in.1, f32[16,384]{1,0:T(8,128)} %inflow_in.1, ...), custom_call_target="tpu_custom_call" | custom-call | tf_op jit(solution)/shard_map/pallas_call | solution.py:329
  30.4 1.4 %shard_map.148 = (f32[16,384]{1,0:T(8,128)}, f32[16,384]{1,0:T(8,128)}, f32[16,384]{1,0:T(8,128)}, f32[4,768]{1,0:T(4,128)}) custom-call(f32[16,384]{1,0:T(8,128)} %get-tuple-element.8.refs_0_, f32[16,384]{1,0:T(8,128)} %get-tuple-element.9.refs_1_, f32[16,384]{1,0:T(8,128)} %get-tuple-element.10.refs_2_, f32[4,768]{1,0:T(4,128)} %get-tuple-element.11.refs_3_), custom_call_target="tpu_custom_call" | custom-call | tf_op jit(solution)/shard_map/pallas_call | solution.py:365
